TPU v7x, 1024 devices: a whole 8x8x8 slice. The times are simulated.
1024 devices in a mesh: fsdp: 128 (over y, z, core), grp: 8 (over x).
Axes of the slice: x: 8, y: 8, z: 8, core: 2. Of those that a mesh axis runs over, the one named last changes fastest.
Arguments:
- gradient: bfloat16 [8, 2560, 4096], P(None, 'fsdp', 'grp'), may hold values from -32 to 32
- momentum: float32 [8, 2560, 4096], P(None, 'fsdp', 'grp'), may hold values from -6 to 6
- row_counts: int32 [8, 128], replicated, may hold values from 1 to 20, 2048 in all within a row
Outputs:
- new_momentum: float32 [8, 2560, 4096], P(None, 'fsdp', 'grp')
- update: float32 [8, 2560, 4096], P(None, 'fsdp', 'grp')
Inputs may be any that keep to these rules, and one draw needn't show every extreme that they name: For each matrix the counts over all owners sum to 2048; owner f holds its rows of matrix m in slots 0 to row_counts[m, f] - 1.
All inputs are finite; a program needn't handle non-finite values.
Results may differ from a plain program's by a relative error of at most 0.023.
Values may be sent and summed in bfloat16 or wider, within the bound.
A program may use at most 32 MiB of HBM per device.

v0:
```python
import math

import jax
import jax.numpy as jnp
from jax import lax
from jax.sharding import PartitionSpec as P

D = 4096
H = 2048


keep_rate = 0.95
first_coef = 1.875
third_coef = -1.25
fifth_coef = 0.375
tiny_value = 1e-06


def from_behind(x, axis, by):
    count = lax.axis_size(axis)
    return lax.ppermute(x, axis, [(i, (i + by) % count) for i in range(count)])


def partner_2(block, axis, apart):
    count = lax.axis_size(axis)
    route = []
    for low in range(count):
        high = low | 1 << apart
        if high != low and high < count:
            route += [(low, high), (high, low)]
    return lax.ppermute(block, axis, route)


def start_rows(row_counts):
    before = jnp.cumsum(row_counts, axis=1) - row_counts
    return before


def slot_targets(starts, counts, capacity, height):
    within = jnp.arange(capacity, dtype=jnp.int32)[None, :]
    target = starts[:, None] + within
    return jnp.where(within < counts[:, None], target, height).reshape(-1)


def spread(shard_piece, bit_list, position, swapper):
    collected = shard_piece[None]
    for bit_index in bit_list:
        partner = swapper(collected, bit_index)
        upper_half = position // (1 << bit_index) % 2
        collected = jnp.where(
            upper_half == 0,
            jnp.concatenate([collected, partner], 0),
            jnp.concatenate([partner, collected], 0),
        )
    return collected


def on_device(gradient, momentum, row_counts):
    new_momentum = keep_rate * momentum + gradient.astype(jnp.float32)
    nesterov = (gradient.astype(jnp.float32) + keep_rate * new_momentum).astype(jnp.bfloat16)
    matrices, capacity, columns = gradient.shape
    owners = lax.axis_size("fsdp")
    position = lax.axis_index("fsdp")
    members = owners // matrices
    level_count = members.bit_length() - 1
    member_bits = list(range(level_count))
    chosen = position // members % matrices
    first_device = chosen * members
    unit_step = 1
    starts = start_rows(row_counts)
    my_starts = jnp.take(starts, chosen, axis=0)
    my_counts = jnp.take(row_counts, chosen, axis=0)
    steps_back = jnp.arange(matrices, dtype=jnp.int32) * members
    arrived = [jnp.take(nesterov, chosen, axis=0)]
    for hop_count in range(1, matrices):
        receiver = (position + hop_count * members) % owners
        outgoing = jnp.take(nesterov, receiver // members % matrices, axis=0)
        arrived.append(from_behind(outgoing, "fsdp", hop_count * members))
    own_slots = jnp.stack(arrived)
    own_owners = (position - steps_back) % owners
    slot_index = jnp.arange(capacity, dtype=jnp.int32)
    live_rows = slot_index[None, :] < jnp.take(my_counts, own_owners)[:, None]
    own_slots = jnp.where(live_rows[:, :, None], own_slots, jnp.zeros_like(own_slots))

    def pair_rows(block_rows, bit_index):
        return partner_2(block_rows, "fsdp", bit_index)

    gathered = spread(own_slots, member_bits, position, pair_rows)
    member_ids = first_device + jnp.arange(members, dtype=jnp.int32) * unit_step
    all_owners = (member_ids[:, None] - steps_back[None, :]) % owners
    flat_owners = all_owners.reshape(-1)
    targets = slot_targets(
        jnp.take(my_starts, flat_owners), jnp.take(my_counts, flat_owners), capacity, H
    )
    full_rows = (
        jnp.zeros((H, columns), jnp.bfloat16)
        .at[targets]
        .set(gathered.reshape(-1, columns), mode="drop")
    )
    slot_rows = own_slots.reshape(-1, columns)
    partial_value = lax.dot_general(
        slot_rows, full_rows, (((1,), (1,)), ((), ())), preferred_element_type=jnp.float32
    )
    gram_rows = lax.psum(partial_value.astype(jnp.bfloat16), "grp").astype(jnp.float32)
    square_part = jnp.sum(gram_rows * gram_rows)
    slot_vector = jnp.where(jnp.arange(matrices, dtype=jnp.int32) == chosen, square_part, 0.0)
    square_sum = jnp.take(lax.psum(slot_vector, "fsdp"), chosen)
    factor = lax.rsqrt(jnp.sqrt(square_sum / H + tiny_value))
    scaled = (gram_rows * (factor * factor)).astype(jnp.bfloat16)
    image_rows = jnp.dot(scaled, full_rows, preferred_element_type=jnp.float32).astype(jnp.bfloat16)
    image_gathered = spread(
        image_rows.reshape(matrices, capacity, columns), member_bits, position, pair_rows
    )
    image_full = (
        jnp.zeros((H, columns), jnp.bfloat16)
        .at[targets]
        .set(image_gathered.reshape(-1, columns), mode="drop")
    )
    second_image = jnp.dot(scaled, image_full, preferred_element_type=jnp.float32)
    combined = (
        first_coef * slot_rows.astype(jnp.float32)
        + third_coef * image_rows.astype(jnp.float32)
        + fifth_coef * second_image
    )
    result = (math.sqrt(D) * factor * combined).reshape(matrices, capacity, columns)
    update = jnp.zeros((matrices, capacity, columns), jnp.float32)
    update = update.at[chosen].set(result[0])
    for hop_count in range(1, matrices):
        returned = from_behind(
            result[hop_count].astype(jnp.bfloat16), "fsdp", owners - hop_count * members
        ).astype(jnp.float32)
        sender = (position + hop_count * members) % owners
        update = update.at[sender // members % matrices].set(returned)
    return (new_momentum, update)


def solution(mesh):
    placed = (P(None, "fsdp", "grp"), P(None, "fsdp", "grp"), P())
    return jax.shard_map(
        on_device,
        mesh=mesh,
        in_specs=placed,
        out_specs=(P(None, "fsdp", "grp"), P(None, "fsdp", "grp")),
        check_vma=False,
    )
```

profile of v0, /device:TPU:1, one launch (start us, length us, event | category | flops | bytes accessed | tf_op | source)
XLA Modules:
  0.0 696.6 jit_solution(15017289930990492098)
XLA Ops:
  9.0 4.1 collective-permute-start
  13.2 4.4 collective-permute-start.1
  17.7 5.0 collective-permute-start.2
  22.6 3.1 collective-permute-start.3
  25.7 5.4 collective-permute-start.4
  32.3 4.7 collective-permute-start.5
  37.1 2.9 collective-permute-start.6
  41.7 12.5 %collective-permute-start.7 = (bf16[1,8,20,512]{3,2,1,0:T(8,128)(2,1)S(1)}, bf16[1,8,20,512]{3,2,1,0:T(8,128)(2,1)S(1)}, u32[]{:S(2)}, u32[]{:S(2)}) collective-permute-start(bf16[1,8,20,512]{3,2,1,0:T(8,128)(2,1)S(1)} %broadcast_select_fusion), channel_id=1, source_target_pairs={{0,8},{8,0},{16,24},{24,16},{32,40},{40,32},{48,56},{56,48},{64,72... | collective-permute-start | bytes 491528 | tf_op jit(solution)/shard_map/ppermute | solution.py:31
  55.3 1.9 collective-permute-start.8
  59.8 7.8 %collective-permute-done.8 = bf16[2,8,20,512]{3,2,1,0:T(8,128)(2,1)S(1)} collective-permute-done((bf16[2,8,20,512]{3,2,1,0:T(8,128)(2,1)S(1)}, bf16[2,8,20,512]{3,2,1,0:T(8,128)(2,1)S(1)}, u32[]{:S(2)}, u32[]{:S(2)}) %collective-permute-start.8) | collective-permute-done | bytes 327712 | tf_op jit(solution)/shard_map/ppermute | solution.py:31
  67.9 2.4 collective-permute-start.9
  70.8 30.6 %collective-permute-done.9 = bf16[4,8,20,512]{3,1,2,0:T(8,128)(2,1)S(1)} collective-permute-done((bf16[4,8,20,512]{3,1,2,0:T(8,128)(2,1)S(1)}, bf16[4,8,20,512]{3,1,2,0:T(8,128)(2,1)S(1)}, u32[]{:S(2)}, u32[]{:S(2)}) %collective-permute-start.9) | collective-permute-done | bytes 655392 | tf_op jit(solution)/shard_map/ppermute | solution.py:31
  103.5 8.9 %collective-permute-start.10 = (bf16[8,8,20,512]{3,1,2,0:T(8,128)(2,1)}, bf16[8,8,20,512]{3,1,2,0:T(8,128)(2,1)}, u32[]{:S(2)}, u32[]{:S(2)}) collective-permute-start(bf16[8,8,20,512]{3,1,2,0:T(8,128)(2,1)} %copy.22), channel_id=1, source_target_pairs={{0,64},{64,0},{8,72},{72,8},{16,80},{80,16},{24,88},{88,24},{32,96... | collective-permute-start | bytes 3932168 | tf_op jit(solution)/shard_map/ppermute | solution.py:31
  112.5 56.4 %collective-permute-done.10 = bf16[8,8,20,512]{3,1,2,0:T(8,128)(2,1)} collective-permute-done((bf16[8,8,20,512]{3,1,2,0:T(8,128)(2,1)}, bf16[8,8,20,512]{3,1,2,0:T(8,128)(2,1)}, u32[]{:S(2)}, u32[]{:S(2)}) %collective-permute-start.10) | collective-permute-done | bytes 1310752 | tf_op jit(solution)/shard_map/ppermute | solution.py:31
  170.8 2.0 maximum_select_fusion
  172.8 5.2 reshape.812
  178.0 12.7 %scatter_custom_fusion = bf16[2048,512]{1,0:T(8,128)(2,1)S(1)} fusion(s32[2560]{0:T(1024)S(1)} %fusion.20, bf16[2560,512]{1,0:T(8,128)(2,1)} %reshape.812, bf16[]{:T(256)} %constant.528.clone.1), kind=kCustom, calls=%fused_computation.20 | custom fusion | bytes 2097664 | tf_op jit(solution)/shard_map/scatter | solution.py:98
  192.4 78.3 %all-reduce.2.cloned.1.call-done = bf16[160,2048]{1,0:T(8,128)(2,1)} async-done(((bf16[160,2048]{1,0:T(8,128)(2,1)}), bf16[160,2048]{1,0:T(8,128)(2,1)}) %all-reduce.2.cloned.1.call-update) | async-done | bytes 655376 | tf_op jit(solution)/shard_map/psum | solution.py:104
  270.7 2.0 fusion
  273.4 254.3 %psum.15 = f32[8]{0:T(128)S(1)} all-reduce(f32[8]{0:T(128)S(1)} %compare_select_fusion.10), channel_id=1, replica_groups=mesh['fsdp'=128,'grp'=8] {'fsdp'}, use_global_device_ids=true, to_apply=%region_5.9 | all-reduce | flops 8 | bytes 64 | tf_op jit(solution)/shard_map/psum | solution.py:107
  530.7 2.3 collective-permute-start.11
  536.0 10.3 %collective-permute-done.12 = bf16[2,8,20,512]{3,2,1,0:T(8,128)(2,1)S(1)} collective-permute-done((bf16[2,8,20,512]{3,2,1,0:T(8,128)(2,1)S(1)}, bf16[2,8,20,512]{3,2,1,0:T(8,128)(2,1)S(1)}, u32[]{:S(2)}, u32[]{:S(2)}) %collective-permute-start.12) | collective-permute-done | bytes 327712 | tf_op jit(solution)/shard_map/ppermute | solution.py:31
  546.7 2.1 collective-permute-start.13
  548.8 31.3 %collective-permute-done.13 = bf16[4,8,20,512]{3,1,2,0:T(8,128)(2,1)S(1)} collective-permute-done((bf16[4,8,20,512]{3,1,2,0:T(8,128)(2,1)S(1)}, bf16[4,8,20,512]{3,1,2,0:T(8,128)(2,1)S(1)}, u32[]{:S(2)}, u32[]{:S(2)}) %collective-permute-start.13) | collective-permute-done | bytes 655392 | tf_op jit(solution)/shard_map/ppermute | solution.py:31
  585.6 56.7 %collective-permute-done.14 = bf16[8,8,20,512]{3,1,2,0:T(8,128)(2,1)S(1)} collective-permute-done((bf16[8,8,20,512]{3,1,2,0:T(8,128)(2,1)S(1)}, bf16[8,8,20,512]{3,1,2,0:T(8,128)(2,1)S(1)}, u32[]{:S(2)}, u32[]{:S(2)}) %collective-permute-start.14) | collective-permute-done | bytes 1310752 | tf_op jit(solution)/shard_map/ppermute | solution.py:31
  643.6 2.2 reshape.820
  645.8 12.7 %scatter_custom_fusion.1 = bf16[2048,512]{1,0:T(8,128)(2,1)S(1)} fusion(s32[2560]{0:T(1024)S(1)} %fusion.20, bf16[2560,512]{1,0:T(8,128)(2,1)} %reshape.820, bf16[]{:T(256)} %constant.528.clone.1), kind=kCustom, calls=%fused_computation.18 | custom fusion | bytes 2097664 | tf_op jit(solution)/shard_map/scatter | solution.py:117
  663.0 5.0 collective-permute-start.17
  668.0 4.5 collective-permute-start.18
  672.4 2.6 collective-permute-start.19
  675.8 5.2 collective-permute-start.20
  681.6 3.4 collective-permute-start.21
  (103 shorter events, 37.5 us)
Async XLA Ops:
  7.2 24.1 %copy-start.1 = (s32[8,128]{1,0:T(8,128)S(1)}, s32[8,128]{1,0:T(8,128)}, u32[]{:S(2)}) copy-start(s32[8,128]{1,0:T(8,128)} %param.27) | copy-start | bytes 12292
  7.2 263.6 %all-reduce.2.cloned.1.call-start = ((), (), s32[]{:S(2)}) async-start(), calls=%async_computation | async-start | bytes 1310720 | tf_op jit(solution)/shard_map/psum | solution.py:104
  9.0 23.2 %collective-permute-start = (bf16[20,512]{1,0:T(8,128)(2,1)S(1)}, bf16[20,512]{1,0:T(8,128)(2,1)S(1)}, u32[]{:S(2)}, u32[]{:S(2)}) collective-permute-start(bf16[20,512]{1,0:T(8,128)(2,1)S(1)} %get-tuple-element.157), channel_id=1, source_target_pairs={{0,128},{8,136},{16,144},{24,152},{32,160},{40,168},{48,176},{56,1... | collective-permute-start | bytes 61448 | tf_op jit(solution)/shard_map/ppermute | solution.py:21
  13.2 23.9 %collective-permute-start.1 = (bf16[20,512]{1,0:T(8,128)(2,1)S(1)}, bf16[20,512]{1,0:T(8,128)(2,1)S(1)}, u32[]{:S(2)}, u32[]{:S(2)}) collective-permute-start(bf16[20,512]{1,0:T(8,128)(2,1)S(1)} %get-tuple-element.156), channel_id=1, source_target_pairs={{0,256},{8,264},{16,272},{24,280},{32,288},{40,296},{48,304},{56,3... | collective-permute-start | bytes 61448 | tf_op jit(solution)/shard_map/ppermute | solution.py:21
  17.7 22.3 %collective-permute-start.2 = (bf16[20,512]{1,0:T(8,128)(2,1)S(1)}, bf16[20,512]{1,0:T(8,128)(2,1)S(1)}, u32[]{:S(2)}, u32[]{:S(2)}) collective-permute-start(bf16[20,512]{1,0:T(8,128)(2,1)S(1)} %get-tuple-element.155), channel_id=1, source_target_pairs={{0,384},{8,392},{16,400},{24,408},{32,416},{40,424},{48,432},{56,4... | collective-permute-start | bytes 61448 | tf_op jit(solution)/shard_map/ppermute | solution.py:21
  22.6 17.3 %collective-permute-start.3 = (bf16[20,512]{1,0:T(8,128)(2,1)S(1)}, bf16[20,512]{1,0:T(8,128)(2,1)S(1)}, u32[]{:S(2)}, u32[]{:S(2)}) collective-permute-start(bf16[20,512]{1,0:T(8,128)(2,1)S(1)} %get-tuple-element.154), channel_id=1, source_target_pairs={{0,512},{8,520},{16,528},{24,536},{32,544},{40,552},{48,560},{56,5... | collective-permute-start | bytes 61448 | tf_op jit(solution)/shard_map/ppermute | solution.py:21
  25.7 14.3 %collective-permute-start.4 = (bf16[20,512]{1,0:T(8,128)(2,1)S(1)}, bf16[20,512]{1,0:T(8,128)(2,1)S(1)}, u32[]{:S(2)}, u32[]{:S(2)}) collective-permute-start(bf16[20,512]{1,0:T(8,128)(2,1)S(1)} %get-tuple-element.153), channel_id=1, source_target_pairs={{0,640},{8,648},{16,656},{24,664},{32,672},{40,680},{48,688},{56,6... | collective-permute-start | bytes 61448 | tf_op jit(solution)/shard_map/ppermute | solution.py:21
  32.3 7.7 %collective-permute-start.5 = (bf16[20,512]{1,0:T(8,128)(2,1)S(1)}, bf16[20,512]{1,0:T(8,128)(2,1)S(1)}, u32[]{:S(2)}, u32[]{:S(2)}) collective-permute-start(bf16[20,512]{1,0:T(8,128)(2,1)S(1)} %get-tuple-element.152), channel_id=1, source_target_pairs={{0,768},{8,776},{16,784},{24,792},{32,800},{40,808},{48,816},{56,8... | collective-permute-start | bytes 61448 | tf_op jit(solution)/shard_map/ppermute | solution.py:21
  37.1 4.6 collective-permute-start.6
  41.7 13.5 %collective-permute-start.7 = (bf16[1,8,20,512]{3,2,1,0:T(8,128)(2,1)S(1)}, bf16[1,8,20,512]{3,2,1,0:T(8,128)(2,1)S(1)}, u32[]{:S(2)}, u32[]{:S(2)}) collective-permute-start(bf16[1,8,20,512]{3,2,1,0:T(8,128)(2,1)S(1)} %broadcast_select_fusion), channel_id=1, source_target_pairs={{0,8},{8,0},{16,24},{24,16},{32,40},{40,32},{48,56},{56,48},{64,72... | collective-permute-start | bytes 491528 | tf_op jit(solution)/shard_map/ppermute | solution.py:31
  55.3 12.2 %collective-permute-start.8 = (bf16[2,8,20,512]{3,2,1,0:T(8,128)(2,1)S(1)}, bf16[2,8,20,512]{3,2,1,0:T(8,128)(2,1)S(1)}, u32[]{:S(2)}, u32[]{:S(2)}) collective-permute-start(bf16[2,8,20,512]{3,2,1,0:T(8,128)(2,1)S(1)} %maximum_select_fusion.6), channel_id=1, source_target_pairs={{0,16},{16,0},{8,24},{24,8},{32,48},{48,32},{40,56},{56,40},{64,80... | collective-permute-start | bytes 983048 | tf_op jit(solution)/shard_map/ppermute | solution.py:31
  67.9 33.4 %collective-permute-start.9 = (bf16[4,8,20,512]{3,1,2,0:T(8,128)(2,1)S(1)}, bf16[4,8,20,512]{3,1,2,0:T(8,128)(2,1)S(1)}, u32[]{:S(2)}, u32[]{:S(2)}) collective-permute-start(bf16[4,8,20,512]{3,1,2,0:T(8,128)(2,1)S(1)} %copy.19), channel_id=1, source_target_pairs={{0,32},{32,0},{8,40},{40,8},{16,48},{48,16},{24,56},{56,24},{64,96... | collective-permute-start | bytes 1966088 | tf_op jit(solution)/shard_map/ppermute | solution.py:31
  103.5 65.5 %collective-permute-start.10 = (bf16[8,8,20,512]{3,1,2,0:T(8,128)(2,1)}, bf16[8,8,20,512]{3,1,2,0:T(8,128)(2,1)}, u32[]{:S(2)}, u32[]{:S(2)}) collective-permute-start(bf16[8,8,20,512]{3,1,2,0:T(8,128)(2,1)} %copy.22), channel_id=1, source_target_pairs={{0,64},{64,0},{8,72},{72,8},{16,80},{80,16},{24,88},{88,24},{32,96... | collective-permute-start | bytes 3932168 | tf_op jit(solution)/shard_map/ppermute | solution.py:31
  530.7 3.3 collective-permute-start.11
  534.1 12.2 %collective-permute-start.12 = (bf16[2,8,20,512]{3,2,1,0:T(8,128)(2,1)S(1)}, bf16[2,8,20,512]{3,2,1,0:T(8,128)(2,1)S(1)}, u32[]{:S(2)}, u32[]{:S(2)}) collective-permute-start(bf16[2,8,20,512]{3,2,1,0:T(8,128)(2,1)S(1)} %maximum_select_fusion.7), channel_id=1, source_target_pairs={{0,16},{16,0},{8,24},{24,8},{32,48},{48,32},{40,56},{56,40},{64,80... | collective-permute-start | bytes 983048 | tf_op jit(solution)/shard_map/ppermute | solution.py:31
  546.7 33.4 %collective-permute-start.13 = (bf16[4,8,20,512]{3,1,2,0:T(8,128)(2,1)S(1)}, bf16[4,8,20,512]{3,1,2,0:T(8,128)(2,1)S(1)}, u32[]{:S(2)}, u32[]{:S(2)}) collective-permute-start(bf16[4,8,20,512]{3,1,2,0:T(8,128)(2,1)S(1)} %copy.25), channel_id=1, source_target_pairs={{0,32},{32,0},{8,40},{40,8},{16,48},{48,16},{24,56},{56,24},{64,96... | collective-permute-start | bytes 1966088 | tf_op jit(solution)/shard_map/ppermute | solution.py:31
  580.7 3.3 copy-start.2
  581.2 61.2 %collective-permute-start.14 = (bf16[8,8,20,512]{3,1,2,0:T(8,128)(2,1)S(1)}, bf16[8,8,20,512]{3,1,2,0:T(8,128)(2,1)S(1)}, u32[]{:S(2)}, u32[]{:S(2)}) collective-permute-start(bf16[8,8,20,512]{3,1,2,0:T(8,128)(2,1)S(1)} %copy.28), channel_id=1, source_target_pairs={{0,64},{64,0},{8,72},{72,8},{16,80},{80,16},{24,88},{88,24},{32,96... | collective-permute-start | bytes 3932168 | tf_op jit(solution)/shard_map/ppermute | solution.py:31
  645.8 12.8 %copy-start = (bf16[160,2048]{1,0:T(8,128)(2,1)S(1)}, bf16[160,2048]{1,0:T(8,128)(2,1)}, u32[]{:S(2)}) copy-start(bf16[160,2048]{1,0:T(8,128)(2,1)} %all-reduce.2.cloned.1.call-done) | copy-start | bytes 1966084
  659.1 16.6 %collective-permute-start.15 = (bf16[20,512]{1,0:T(8,128)(2,1)S(1)}, bf16[20,512]{1,0:T(8,128)(2,1)S(1)}, u32[]{:S(2)}, u32[]{:S(2)}) collective-permute-start(bf16[20,512]{1,0:T(8,128)(2,1)S(1)} %get-tuple-element.164), channel_id=1, source_target_pairs={{0,896},{8,904},{16,912},{24,920},{32,928},{40,936},{48,944},{56,9... | collective-permute-start | bytes 61448 | tf_op jit(solution)/shard_map/ppermute | solution.py:21
  661.0 20.6 %collective-permute-start.16 = (bf16[20,512]{1,0:T(8,128)(2,1)S(1)}, bf16[20,512]{1,0:T(8,128)(2,1)S(1)}, u32[]{:S(2)}, u32[]{:S(2)}) collective-permute-start(bf16[20,512]{1,0:T(8,128)(2,1)S(1)} %get-tuple-element.163), channel_id=1, source_target_pairs={{0,768},{8,776},{16,784},{24,792},{32,800},{40,808},{48,816},{56,8... | collective-permute-start | bytes 61448 | tf_op jit(solution)/shard_map/ppermute | solution.py:21
  663.0 22.7 %collective-permute-start.17 = (bf16[20,512]{1,0:T(8,128)(2,1)S(1)}, bf16[20,512]{1,0:T(8,128)(2,1)S(1)}, u32[]{:S(2)}, u32[]{:S(2)}) collective-permute-start(bf16[20,512]{1,0:T(8,128)(2,1)S(1)} %get-tuple-element.162), channel_id=1, source_target_pairs={{0,640},{8,648},{16,656},{24,664},{32,672},{40,680},{48,688},{56,6... | collective-permute-start | bytes 61448 | tf_op jit(solution)/shard_map/ppermute | solution.py:21
  668.0 18.3 %collective-permute-start.18 = (bf16[20,512]{1,0:T(8,128)(2,1)S(1)}, bf16[20,512]{1,0:T(8,128)(2,1)S(1)}, u32[]{:S(2)}, u32[]{:S(2)}) collective-permute-start(bf16[20,512]{1,0:T(8,128)(2,1)S(1)} %get-tuple-element.161), channel_id=1, source_target_pairs={{0,512},{8,520},{16,528},{24,536},{32,544},{40,552},{48,560},{56,5... | collective-permute-start | bytes 61448 | tf_op jit(solution)/shard_map/ppermute | solution.py:21
  672.4 14.5 %collective-permute-start.19 = (bf16[20,512]{1,0:T(8,128)(2,1)S(1)}, bf16[20,512]{1,0:T(8,128)(2,1)S(1)}, u32[]{:S(2)}, u32[]{:S(2)}) collective-permute-start(bf16[20,512]{1,0:T(8,128)(2,1)S(1)} %get-tuple-element.160), channel_id=1, source_target_pairs={{0,384},{8,392},{16,400},{24,408},{32,416},{40,424},{48,432},{56,4... | collective-permute-start | bytes 61448 | tf_op jit(solution)/shard_map/ppermute | solution.py:21
  675.8 11.8 %collective-permute-start.20 = (bf16[20,512]{1,0:T(8,128)(2,1)S(1)}, bf16[20,512]{1,0:T(8,128)(2,1)S(1)}, u32[]{:S(2)}, u32[]{:S(2)}) collective-permute-start(bf16[20,512]{1,0:T(8,128)(2,1)S(1)} %get-tuple-element.159), channel_id=1, source_target_pairs={{0,256},{8,264},{16,272},{24,280},{32,288},{40,296},{48,304},{56,3... | collective-permute-start | bytes 61448 | tf_op jit(solution)/shard_map/ppermute | solution.py:21
  681.6 6.5 collective-permute-start.21
Sparse Core Ops, SparseCore 0:
  192.6 78.1 all-reduce.1
where the time goes:
time: 700 us; the launch traced here: 697 us
  waiting for transfers between devices  275 us (39%)
  blocking collectives  254 us (36%)
  starting transfers between devices  88.2 us (13%)
  local copies, waits for them, and re-layouts  44 us (6%)
  between operations  16 us (2%)
  other arithmetic  15.4 us (2%)
    psum x1, blocking collectives, on_device(): square_sum = jnp.take(lax.psum(slot_vector, 'fsdp'), chosen)  254 us
    ppermute x8, waiting for transfers between devices, partner_2(): return lax.ppermute(block, axis, route)  195 us
    psum x1, waiting for transfers between devices, on_device(): lax.psum(partial_value.astype(jnp.bfloat16), 'grp').astype(jnp.float32)  78.3 us
    ppermute x14, starting transfers between devices, from_behind(): return lax.ppermute(x, axis, [(i, (i + by) % count) for i in range(count)])  54.2 us
    ppermute x8, starting transfers between devices, partner_2(): return lax.ppermute(block, axis, route)  34 us
  transfers between devices with their start and end apart: 23, of which 10 were waited for; matrix products, arithmetic and copies ran while one was open for 2% of the time, Pallas kernels for 0%

commit v1 on v0

v1 whole, which is shorter than its diff:
```python
import math

import jax
import jax.numpy as jnp
from jax import lax
from jax.experimental import pallas as pl
from jax.experimental.pallas import tpu as pltpu
from jax.sharding import PartitionSpec as P

D = 4096
H = 2048

keep_rate = 0.95
first_coef = 1.875
third_coef = -1.25
fifth_coef = 0.375
tiny_value = 1e-06

MESH = pl.DeviceIdType.MESH
RING = 8
COLS = 512
WIDE = 640
ROWS = 160
HALF = ROWS // 2
CHUNK = 4 * ROWS
CHUNKS = 4
FULL = CHUNK * CHUNKS
PLACE = {0: 0, -1: 1, 1: 2, -2: 3, 2: 4, -3: 5, 3: 6, 4: 7}
F32 = jnp.float32
BF16 = jnp.bfloat16


def one_hot(k):
    r = lax.broadcasted_iota(jnp.int32, (32, 128), 0)
    c = lax.broadcasted_iota(jnp.int32, (32, 128), 1)
    return jnp.where(c == 16 * (r // 4) + 4 * k + r % 4, 1.0, 0.0).astype(BF16)


def one_hot_back(k):
    r = lax.broadcasted_iota(jnp.int32, (128, 32), 1)
    c = lax.broadcasted_iota(jnp.int32, (128, 32), 0)
    return jnp.where(c == 16 * (r // 4) + 4 * k + r % 4, 1.0, 0.0).astype(BF16)


def kernel(
    u_ref,
    out_ref,
    arrived,
    u_all,
    v_all,
    stage,
    got,
    got_rest,
    gram,
    w_acc,
    squares,
    reply,
    returned,
    send_sems,
    owner_sem,
    ring_u,
    sib_u,
    ring_v,
    sib_v,
    got_sem,
    rest_sem,
    spread_sem,
    square_sem,
    return_sem,
):
    f = lax.axis_index("fsdp")
    x = lax.axis_index("grp")
    y = f // 16
    z = (f // 2) % 8
    core = f % 2
    sibling = (f + 1 - 2 * core, x)

    def at_y(by):
        return (((y + by) % 8) * 16 + z * 2 + core, x)

    def at_z(by):
        return (y * 16 + ((z + by) % 8) * 2 + core, x)

    def at_x(by):
        return (f, (x + by) % 8)

    def push(src, dst, send_sem, recv_sem, device):
        pltpu.make_async_remote_copy(
            src_ref=src,
            dst_ref=dst,
            send_sem=send_sem,
            recv_sem=recv_sem,
            device_id=device,
            device_id_type=MESH,
        ).start()

    def wait(ref, sem):
        pltpu.make_async_copy(ref, ref, sem).wait()

    barrier = pltpu.get_barrier_semaphore()
    for by in range(1, 8):
        for peer in (at_y(by), at_z(by), at_x(by)):
            pl.semaphore_signal(barrier, inc=1, device_id=peer, device_id_type=MESH)
    pl.semaphore_signal(barrier, inc=1, device_id=sibling, device_id_type=MESH)
    pl.semaphore_wait(barrier, 22)

    for by in range(1, 8):
        push(u_ref.at[(y + by) % 8], arrived.at[by], send_sems.at[0], owner_sem, at_y(by))
    arrived[0] = u_ref[y]
    wait(arrived.at[pl.ds(1, 7)], owner_sem)
    for d in range(8):
        u_all[16 * d : 16 * d + 16, :] = arrived[d, :, :COLS]
    packed = arrived[:, :, COLS:].reshape(128, 128)
    for k in range(4):
        u_all[128:160, 128 * k : 128 * k + 128] = jnp.dot(
            one_hot(k), packed, preferred_element_type=F32
        ).astype(BF16)

    def gather(buf, ring_sem, sib_sem, ring_send, sib_send, on_chunk):
        def part(place, half):
            return buf.at[pl.ds(2 * ROWS * place + HALF * half, HALF)]

        def twin(place, half):
            return buf.at[pl.ds(2 * ROWS * place + ROWS + HALF * half, HALF)]

        def place_of(way, hop):
            return PLACE[4 if hop == 4 else (-hop if way == 0 else hop)]

        for half in range(2):
            for way in range(2):
                push(
                    part(0, half),
                    part(place_of(way, 1), half),
                    ring_send,
                    ring_sem.at[way, 0, half],
                    at_z(1 if way == 0 else -1),
                )
            push(part(0, half), twin(0, half), sib_send, sib_sem.at[0], sibling)
        for hop in range(1, 5):
            for half in range(2):
                for way in range(2):
                    if hop == 4 and half != way:
                        continue
                    here = place_of(way, hop)
                    wait(part(here, half), ring_sem.at[way, hop - 1, half])
                    if hop < 3 or (hop == 3 and half == way):
                        push(
                            part(here, half),
                            part(place_of(way, hop + 1), half),
                            ring_send,
                            ring_sem.at[way, hop, half],
                            at_z(1 if way == 0 else -1),
                        )
                    push(part(here, half), twin(here, half), sib_send, sib_sem.at[here], sibling)
            a = hop - 1
            for place in (2 * a, 2 * a + 1):
                wait(buf.at[pl.ds(2 * ROWS * place + ROWS, ROWS)], sib_sem.at[place])
            on_chunk(a)

    own_rows = pl.ds(pl.multiple_of(16 * x, 16), 16)

    def reduce_chunk(a):
        wait(got.at[a, pl.ds(1, 7)], got_sem.at[a])
        total = stage[a, x].astype(F32)
        for by in range(1, 8):
            total += got[a, by].astype(F32)
        gram[a, own_rows, :] = total.astype(BF16)

    def piece(kind, owner):
        if kind == 2:
            return gram.at[owner // 2, pl.ds(pl.multiple_of(128 + 16 * (owner % 2), 16), 16)]
        return gram.at[pl.ds(2 * kind, 2), pl.ds(pl.multiple_of(16 * owner, 16), 16)]

    def spread_own(kind):
        for way in range(2):
            push(
                piece(kind, x),
                piece(kind, x),
                send_sems.at[6 + kind],
                spread_sem.at[way, 0, kind],
                at_x(1 if way == 0 else -1),
            )

    def spread_hop(kind, hop):
        last_way = (0, 1, 0)[kind]
        for way in range(2):
            if hop == 4 and way != last_way:
                continue
            owner = (x - hop) % 8 if way == 0 else (x + hop) % 8
            wait(piece(kind, owner), spread_sem.at[way, hop - 1, kind])
            if hop < 3 or (hop == 3 and way == last_way):
                push(
                    piece(kind, owner),
                    piece(kind, owner),
                    send_sems.at[6 + kind],
                    spread_sem.at[way, hop, kind],
                    at_x(1 if way == 0 else -1),
                )

    def gram_chunk(a):
        product = lax.dot_general(
            u_all[0:ROWS, :],
            u_all[CHUNK * a : CHUNK * a + CHUNK, :],
            (((1,), (1,)), ((), ())),
            preferred_element_type=F32,
        )
        stage[a] = product.astype(BF16).reshape(10, 16, CHUNK)
        for by in range(1, 8):
            push(
                stage.at[a, (x + by) % 8],
                got.at[a, by],
                send_sems.at[5],
                got_sem.at[a],
                at_x(by),
            )
        if a == 2:
            reduce_chunk(0)
            reduce_chunk(1)
            spread_own(0)

    gather(u_all, ring_u, sib_u, send_sems.at[1], send_sems.at[2], gram_chunk)
    for by in range(1, 8):
        owner = (x + by) % 8
        push(
            stage.at[owner // 2, 8 + owner % 2],
            got_rest.at[by],
            send_sems.at[5],
            rest_sem,
            at_x(by),
        )
    spread_hop(0, 1)
    reduce_chunk(2)
    reduce_chunk(3)
    spread_own(1)
    wait(got_rest.at[pl.ds(1, 7)], rest_sem)
    total = stage[x // 2, 8 + x % 2].astype(F32)
    for by in range(1, 8):
        total += got_rest[by].astype(F32)
    gram[x // 2, pl.ds(pl.multiple_of(128 + 16 * (x % 2), 16), 16), :] = total.astype(BF16)
    spread_own(2)
    spread_hop(0, 2)
    spread_hop(1, 1)
    spread_hop(2, 1)
    spread_hop(0, 3)
    spread_hop(1, 2)
    spread_hop(2, 2)
    spread_hop(0, 4)
    spread_hop(1, 3)
    spread_hop(2, 3)
    spread_hop(1, 4)
    spread_hop(2, 4)

    image = jnp.zeros((ROWS, COLS), F32)
    for a in range(CHUNKS):
        image += jnp.dot(
            gram[a], u_all[CHUNK * a : CHUNK * a + CHUNK, :], preferred_element_type=F32
        )
    v_all[0:ROWS, :] = image.astype(BF16)

    def image_chunk(a):
        product = jnp.dot(
            gram[a], v_all[CHUNK * a : CHUNK * a + CHUNK, :], preferred_element_type=F32
        )
        if a == 0:
            w_acc[...] = product
        else:
            w_acc[...] += product
        if a == 0:
            sums = jnp.zeros((8, 128), F32)
            for b in range(CHUNKS):
                rows = gram[b].astype(F32)
                part = jnp.sum((rows * rows).reshape(20, 8, CHUNK), axis=0)
                for k in range(CHUNK // 128):
                    sums += part[:, 128 * k : 128 * k + 128]
            squares[0] = sums
            push(squares.at[0], squares.at[1], send_sems.at[9], square_sem.at[0], sibling)
        if a == 1:
            wait(squares.at[1], square_sem.at[0])
            squares[2] = squares[0] + squares[1]
            for by in range(1, 8):
                push(squares.at[2], squares.at[2 + by], send_sems.at[10], square_sem.at[1], at_z(by))

    gather(v_all, ring_v, sib_v, send_sems.at[3], send_sems.at[4], image_chunk)
    wait(squares.at[pl.ds(3, 7)], square_sem.at[1])
    total = squares[2]
    for by in range(1, 8):
        total += squares[2 + by]
    square_sum = jnp.sum(total, keepdims=True)
    factor = lax.rsqrt(jnp.sqrt(square_sum / H + tiny_value))
    factor_2 = factor * factor
    result = (math.sqrt(D) * factor) * (
        first_coef * u_all[0:ROWS, :].astype(F32)
        + (third_coef * factor_2) * v_all[0:ROWS, :].astype(F32)
        + (fifth_coef * factor_2 * factor_2) * w_acc[...]
    )
    result = result.astype(BF16)
    for d in range(8):
        reply[d, :, :COLS] = result[16 * d : 16 * d + 16, :]
    packed = jnp.zeros((128, 128), F32)
    for k in range(4):
        packed += jnp.dot(
            one_hot_back(k),
            result[128:160, 128 * k : 128 * k + 128],
            preferred_element_type=F32,
        )
    reply[:, :, COLS:] = packed.astype(BF16).reshape(8, 16, 128)
    for by in range(1, 8):
        push(reply.at[by], returned.at[y], send_sems.at[11], return_sem, at_y(-by))
    returned[y] = reply[0]
    wait(returned.at[pl.ds(0, 7)], return_sem)
    out_ref[...] = returned[...]

    wait(arrived.at[pl.ds(1, 7)], send_sems.at[0])
    wait(u_all.at[pl.ds(0, 7 * ROWS)], send_sems.at[1])
    wait(u_all.at[pl.ds(0, 8 * ROWS)], send_sems.at[2])
    wait(v_all.at[pl.ds(0, 7 * ROWS)], send_sems.at[3])
    wait(v_all.at[pl.ds(0, 8 * ROWS)], send_sems.at[4])
    for a in range(CHUNKS):
        wait(got.at[a, pl.ds(1, 7)], send_sems.at[5])
    wait(got_rest.at[pl.ds(1, 7)], send_sems.at[5])
    for kind in range(3):
        for _ in range(7):
            wait(piece(kind, x), send_sems.at[6 + kind])
    wait(squares.at[0], send_sems.at[9])
    wait(squares.at[pl.ds(3, 7)], send_sems.at[10])
    wait(reply.at[pl.ds(1, 7)], send_sems.at[11])


def step(packed):
    DMA = pltpu.SemaphoreType.DMA
    return pl.pallas_call(
        kernel,
        out_shape=jax.ShapeDtypeStruct((8, 16, WIDE), BF16),
        in_specs=[pl.BlockSpec(memory_space=pltpu.VMEM)],
        out_specs=pl.BlockSpec(memory_space=pltpu.VMEM),
        scratch_shapes=[
            pltpu.VMEM((8, 16, WIDE), BF16),
            pltpu.VMEM((FULL, COLS), BF16),
            pltpu.VMEM((FULL, COLS), BF16),
            pltpu.VMEM((CHUNKS, 10, 16, CHUNK), BF16),
            pltpu.VMEM((CHUNKS, 8, 16, CHUNK), BF16),
            pltpu.VMEM((8, 16, CHUNK), BF16),
            pltpu.VMEM((CHUNKS, ROWS, CHUNK), BF16),
            pltpu.VMEM((ROWS, COLS), F32),
            pltpu.VMEM((10, 8, 128), F32),
            pltpu.VMEM((8, 16, WIDE), BF16),
            pltpu.VMEM((8, 16, WIDE), BF16),
            DMA((12,)),
            DMA,
            DMA((2, 4, 2)),
            DMA((8,)),
            DMA((2, 4, 2)),
            DMA((8,)),
            DMA((CHUNKS,)),
            DMA,
            DMA((2, 4, 3)),
            DMA((2,)),
            DMA,
        ],
        compiler_params=pltpu.CompilerParams(
            collective_id=0, has_side_effects=True, vmem_limit_bytes=40 * 1024 * 1024
        ),
    )(packed)


def on_device(gradient, momentum, row_counts):
    new_momentum = keep_rate * momentum + gradient.astype(F32)
    nesterov = (gradient.astype(F32) + keep_rate * new_momentum).astype(BF16)
    matrices, capacity, columns = gradient.shape
    position = lax.axis_index("fsdp")
    counts = jnp.take(row_counts, position, axis=1)
    live = jnp.arange(capacity, dtype=jnp.int32)[None, :] < counts[:, None]
    slots = jnp.where(live[:, :, None], nesterov, jnp.zeros_like(nesterov))
    rest = slots[:, 16:, :].reshape(8, 4, 4, 128).transpose(0, 2, 1, 3).reshape(8, 16, 128)
    packed = jnp.concatenate([slots[:, :16, :], rest], axis=2)
    result = step(packed)
    rest = result[:, :, COLS:].reshape(8, 4, 4, 128).transpose(0, 2, 1, 3).reshape(8, 4, COLS)
    update = jnp.concatenate([result[:, :, :COLS], rest], axis=1).astype(F32)
    return (new_momentum, update)


def solution(mesh):
    placed = (P(None, "fsdp", "grp"), P(None, "fsdp", "grp"), P())
    return jax.shard_map(
        on_device,
        mesh=mesh,
        in_specs=placed,
        out_specs=(P(None, "fsdp", "grp"), P(None, "fsdp", "grp")),
        check_vma=False,
    )
```

time: 700 us -> 105 us (0.15)
  waiting for transfers between devices: 275 us -> 0 us
  blocking collectives: 254 us -> 0 us
  Pallas kernels: 0 us -> 99 us
  starting transfers between devices: 88.2 us -> 0 us
  local copies, waits for them, and re-layouts: 44 us -> 2.64 us
  between operations: 16 us -> 0.72 us
  other arithmetic: 15.4 us -> 1.93 us
    psum x1 -> x0, blocking collectives: 254 us -> none  [on_device(): square_sum = jnp.take(lax.psum(slot_vector, 'fsdp'), chosen)]
    ppermute x22 -> x0, waiting for transfers between devices: 197 us -> none  [the longest x8 195 us: partner_2(): return lax.ppermute(block, axis, route)]
    pallas_call x0 -> x1, Pallas kernels: none -> 99 us  [step(): pl.pallas_call(kernel, out_shape=jax.ShapeDtypeStruct((8, 16, WIDE), BF16...]
    ppermute x22 -> x0, starting transfers between devices: 88.2 us -> none  [the longest x14 54.2 us: from_behind(): return lax.ppermute(x, axis, [(i, (i + by) % count) for i in range(count)])]
    psum x1 -> x0, waiting for transfers between devices: 78.3 us -> none  [on_device(): lax.psum(partial_value.astype(jnp.bfloat16), 'grp').astype(jnp.float32)]
    scatter x2 -> x0, local copies, waits for them, and re-layouts: 25.5 us -> none  [the longest x1 12.7 us: on_device(): image_full = jnp.zeros((H, columns), jnp.bfloat16).at[targets].set(image_...]
    select_n x7 -> x0, local copies, waits for them, and re-layouts: 9.86 us -> none  [the longest x6 9.75 us: spread(): jnp.where(upper_half == 0, jnp.concatenate([collected, partner], 0), jnp....]
  transfers between devices with their start and end apart: 23 -> 0, of which waited for: 10 -> 0; matrix products, arithmetic and copies ran while one was open for 2% -> 0% of each run, Pallas kernels for 0% -> 0%
where the time goes in v1:
time: 105 us; the launch traced here: 104 us
  Pallas kernels  99 us (94%)
  local copies, waits for them, and re-layouts  2.64 us (3%)
  other arithmetic  1.93 us (2%)
    pallas_call x1, Pallas kernels, step(): pl.pallas_call(kernel, out_shape=jax.ShapeDtypeStruct((8, 16, WIDE), BF16...  99 us
    unnamed x8, local copies, waits for them, and re-layouts  2.6 us

profile of v1, /device:TPU:1, one launch (start us, length us, event | category | flops | bytes accessed | tf_op | source)
XLA Modules:
  0.0 104.3 jit_solution(4754162805676252910)
XLA Ops:
  0.6 0.0 copy-start.2
  0.6 0.7 copy-done.2
  1.3 0.2 select_reduce_fusion
  1.5 0.1 iota_compare_fusion
  1.6 1.4 %fusion.1 = bf16[8,20,512]{2,1,0:T(8,128)(2,1)S(1)} fusion(pred[8,20]{1,0:T(8,128)(4,1)S(1)} %iota_compare_fusion, bf16[8,20,512]{2,0,1:T(8,128)(2,1)} %param.3, f32[8,20,512]{2,0,1:T(8,128)} %param.4), kind=kLoop, calls=%fused_computation.4 | loop fusion | flops 573440 | bytes 655520 | tf_op jit(solution)/shard_map/jit(_where)/select_n | solution.py:373
  3.0 99.0 %shard_map.50 = bf16[8,16,640]{2,1,0:T(8,128)(2,1)S(1)} custom-call(bf16[8,16,640]{2,1,0:T(8,128)(2,1)S(1)} %pad_maximum_fusion.u_ref), custom_call_target="tpu_custom_call" | custom-call | tf_op jit(solution)/shard_map/pallas_call | solution.py:331
  102.1 0.0 copy-start
  102.1 0.0 copy-start.1
  102.1 0.9 copy.9
  103.1 0.0 copy-done
  103.1 0.0 copy-done.1
  103.1 0.3 convert_add_fusion.1
  103.4 0.9 copy.8
  (6 shorter events, 0.1 us)
Async XLA Ops:
  0.6 0.7 copy-start.2
  102.1 1.0 copy-start
  102.1 1.0 copy-start.1

commit v2 on v1

v2 whole, which is shorter than its diff:
```python
import math

import jax
import jax.numpy as jnp
from jax import lax
from jax.experimental import pallas as pl
from jax.experimental.pallas import tpu as pltpu
from jax.sharding import PartitionSpec as P

D = 4096
H = 2048

keep_rate = 0.95
first_coef = 1.875
third_coef = -1.25
fifth_coef = 0.375
tiny_value = 1e-06

MESH = pl.DeviceIdType.MESH
COLS = 512
WIDE = 640
ROWS = 160
CHUNK = 4 * ROWS
CHUNKS = 4
FULL = CHUNK * CHUNKS
SUBS = 5
PLACE = {0: 0, -1: 1, 1: 2, -2: 3, 2: 4, -3: 5, 3: 6, 4: 7}
ORDER = (0, 1, 7, 2, 6, 3, 5, 4)
FARTHEST_FIRST = (4, 3, 5, 2, 6, 1, 7)
F32 = jnp.float32
BF16 = jnp.bfloat16


def selection(shape, wanted):
    r = lax.broadcasted_iota(jnp.int32, shape, 0)
    c = lax.broadcasted_iota(jnp.int32, shape, 1)
    return jnp.where(c == wanted(r), 1.0, 0.0).astype(BF16)


def pick(chosen, rows):
    return jnp.dot(chosen, rows, preferred_element_type=F32)


def kernel(
    gradient_ref,
    momentum_ref,
    counts_ref,
    out_ref,
    gradient,
    momentum,
    counts,
    message,
    arrived,
    u_all,
    v_all,
    stage,
    got,
    got_rest,
    gram,
    w_acc,
    squares,
    reply,
    returned,
    local_sem,
    send_sems,
    owner_sem,
    ring_u,
    sib_u,
    ring_v,
    sib_v,
    got_sem,
    rest_sem,
    spread_sem,
    square_sem,
    return_sem,
):
    f = lax.axis_index("fsdp")
    x = lax.axis_index("grp")
    y = f // 16
    z = (f // 2) % 8
    core = f % 2
    sibling = (f + 1 - 2 * core, x)

    def at_y(by):
        return (((y + by) % 8) * 16 + z * 2 + core, x)

    def at_z(by):
        return (y * 16 + ((z + by) % 8) * 2 + core, x)

    def at_x(by):
        return (f, (x + by) % 8)

    def push(src, dst, send_sem, recv_sem, device):
        pltpu.make_async_remote_copy(
            src_ref=src,
            dst_ref=dst,
            send_sem=send_sem,
            recv_sem=recv_sem,
            device_id=device,
            device_id_type=MESH,
        ).start()

    def wait(ref, sem):
        pltpu.make_async_copy(ref, ref, sem).wait()

    barrier = pltpu.get_barrier_semaphore()
    for by in range(1, 8):
        for peer in (at_y(by), at_z(by), at_x(by)):
            pl.semaphore_signal(barrier, inc=1, device_id=peer, device_id_type=MESH)
    pl.semaphore_signal(barrier, inc=1, device_id=sibling, device_id_type=MESH)

    fetches = [
        pltpu.make_async_copy(src, dst, local_sem.at[i])
        for i, (src, dst) in enumerate(
            ((gradient_ref, gradient), (momentum_ref, momentum), (counts_ref, counts))
        )
    ]
    for fetch in fetches:
        fetch.start()
    for fetch in fetches:
        fetch.wait()
    grad = gradient[...].astype(F32)
    rows = grad + keep_rate * (keep_rate * momentum[...] + grad)
    lane = lax.broadcasted_iota(jnp.int32, (8, 128), 1)
    held = jnp.sum(jnp.where(lane == f, counts[...], 0), axis=1, keepdims=True)
    slot = lax.broadcasted_iota(jnp.int32, (20, 8, COLS), 0)
    rows = jnp.where(slot < held[None], rows, 0.0).reshape(ROWS, COLS).astype(BF16)
    main = pick(selection((128, ROWS), lambda r: 8 * (r % 16) + r // 16), rows)
    message[:, :, :COLS] = main.astype(BF16).reshape(8, 16, COLS)
    rest = jnp.zeros((128, 128), F32)
    for k in range(4):
        chosen = selection(
            (128, 32), lambda r: jnp.where(r % 16 // 4 == k, 8 * (r % 4) + r // 16, -1)
        )
        rest += pick(chosen, rows[128:ROWS, 128 * k : 128 * k + 128])
    message[:, :, COLS:] = rest.astype(BF16).reshape(8, 16, 128)

    pl.semaphore_wait(barrier, 22)

    class Ring:
        def __init__(self, buf, parts, ring_sem, sib_sem, ring_send, sib_send):
            self.buf, self.parts = buf, parts
            self.ring_sem, self.sib_sem = ring_sem, sib_sem
            self.ring_send, self.sib_send = ring_send, sib_send

        def refs(self, place, twin, sub):
            base = 2 * ROWS * place + ROWS * twin
            return [
                self.buf.at[pl.ds(start + base if isinstance(start, int) else pl.multiple_of(start + base, 16), size)]
                for start, size in self.parts[sub]
            ]

        def place(self, way, hop):
            return PLACE[4 if hop == 4 else (-hop if way == 0 else hop)]

        def forward(self, way, hop, sub):
            source = 0 if hop == 1 else self.place(way, hop - 1)
            for src, dst in zip(
                self.refs(source, 0, sub), self.refs(self.place(way, hop), 0, sub), strict=True
            ):
                push(
                    src,
                    dst,
                    self.ring_send,
                    self.ring_sem.at[way, hop - 1, sub],
                    at_z(1 if way == 0 else -1),
                )

        def twin(self, place, sub):
            for src, dst in zip(self.refs(place, 0, sub), self.refs(place, 1, sub), strict=True):
                push(src, dst, self.sib_send, self.sib_sem.at[place], sibling)

        def send_own(self, sub):
            for way in range(2):
                self.forward(way, 1, sub)
            self.twin(0, sub)

        def step(self, hop, sub):
            last_way = 0 if sub < 3 else 1
            size = sum(size for _, size in self.parts[sub])
            for way in range(2):
                if hop == 4 and way != last_way:
                    continue
                wait(self.buf.at[pl.ds(0, size)], self.ring_sem.at[way, hop - 1, sub])
                if hop < 3 or (hop == 3 and way == last_way):
                    self.forward(way, hop + 1, sub)
                self.twin(self.place(way, hop), sub)

        def settle(self, a):
            for place in (2 * a, 2 * a + 1):
                wait(self.buf.at[pl.ds(2 * ROWS * place + ROWS, ROWS)], self.sib_sem.at[place])

    group = {q: 16 * ((x + q) % 8) for q in range(-3, 5)}
    whole = Ring(
        u_all,
        [[(0, 16)], [(16, 32)], [(48, 32)], [(80, 48)], [(128, 32)]],
        ring_u,
        sib_u,
        send_sems.at[1],
        send_sems.at[2],
    )
    images = Ring(
        v_all,
        [[(group[0], 16)]]
        + [[(group[q], 16), (group[-q], 16)] for q in (1, 2, 3)]
        + [[(group[4], 16), (128, 32)]],
        ring_v,
        sib_v,
        send_sems.at[3],
        send_sems.at[4],
    )

    own_rows = pl.ds(pl.multiple_of(16 * x, 16), 16)

    def reduce_chunk(a):
        wait(got.at[a, pl.ds(1, 7)], got_sem.at[a])
        total = stage[a, x].astype(F32)
        for by in range(1, 8):
            total += got[a, by].astype(F32)
        gram[a, own_rows, :] = total.astype(BF16)

    def piece(kind, owner):
        if kind == 2:
            return gram.at[owner // 2, pl.ds(pl.multiple_of(128 + 16 * (owner % 2), 16), 16)]
        return gram.at[pl.ds(2 * kind, 2), pl.ds(pl.multiple_of(16 * owner, 16), 16)]

    def spread_own(kind):
        for way in range(2):
            push(
                piece(kind, x),
                piece(kind, x),
                send_sems.at[6 + kind],
                spread_sem.at[way, 0, kind],
                at_x(1 if way == 0 else -1),
            )

    def spread_hop(kind, hop):
        last_way = (0, 1, 0)[kind]
        for way in range(2):
            if hop == 4 and way != last_way:
                continue
            owner = (x - hop) % 8 if way == 0 else (x + hop) % 8
            wait(piece(kind, owner), spread_sem.at[way, hop - 1, kind])
            if hop < 3 or (hop == 3 and way == last_way):
                push(
                    piece(kind, owner),
                    piece(kind, owner),
                    send_sems.at[6 + kind],
                    spread_sem.at[way, hop, kind],
                    at_x(1 if way == 0 else -1),
                )

    def gram_chunk(a):
        whole.settle(a)
        product = lax.dot_general(
            u_all[0:ROWS, :],
            u_all[CHUNK * a : CHUNK * a + CHUNK, :],
            (((1,), (1,)), ((), ())),
            preferred_element_type=F32,
        )
        stage[a] = product.astype(BF16).reshape(10, 16, CHUNK)
        for by in FARTHEST_FIRST:
            push(
                stage.at[a, (x + by) % 8],
                got.at[a, by],
                send_sems.at[5],
                got_sem.at[a],
                at_x(by),
            )
        for half in range(2):
            owner = 2 * a + half

            @pl.when(x != owner)
            def _():
                push(
                    stage.at[a, 8 + half],
                    got_rest.at[(owner - x) % 8],
                    send_sems.at[5],
                    rest_sem,
                    (f, owner),
                )

    for by in FARTHEST_FIRST:
        push(message.at[(y + by) % 8], arrived.at[by], send_sems.at[0], owner_sem.at[by], at_y(by))
    arrived[0] = message[y]
    u_all[0:16, :] = arrived[0, :, :COLS]
    whole.send_own(0)

    def take(first, last):
        for p in range(first, last):
            d = ORDER[p]
            wait(arrived.at[d], owner_sem.at[d])
            u_all[16 * p : 16 * p + 16, :] = arrived[d, :, :COLS]

    take(1, 3)
    whole.send_own(1)
    take(3, 5)
    whole.send_own(2)
    take(5, 8)
    whole.send_own(3)
    packed = arrived[:, :, COLS:].reshape(128, 128)
    for k in range(4):
        chosen = selection((32, 128), lambda r: 16 * (r // 4) + 4 * k + r % 4)
        u_all[128:160, 128 * k : 128 * k + 128] = pick(chosen, packed).astype(BF16)
    whole.send_own(4)
    for hop in range(1, 5):
        for sub in range(SUBS):
            whole.step(hop, sub)
        gram_chunk(hop - 1)
        if hop == 3:
            reduce_chunk(0)
            reduce_chunk(1)
            spread_own(0)

    spread_hop(0, 1)
    reduce_chunk(2)
    reduce_chunk(3)
    spread_own(1)

    def image_of(sub):
        parts = [
            pl.ds(start if isinstance(start, int) else pl.multiple_of(start, 16), size)
            for start, size in images.parts[sub]
        ]
        total = None
        for a in range(CHUNKS):
            left = jnp.concatenate([gram[a, part, :] for part in parts], axis=0)
            product = jnp.dot(
                left, u_all[CHUNK * a : CHUNK * a + CHUNK, :], preferred_element_type=F32
            )
            total = product if total is None else total + product
        total, done = total.astype(BF16), 0
        for part in parts:
            v_all[part, :] = total[done : done + part.size]
            done += part.size
        images.send_own(sub)

    image_of(0)
    wait(got_rest.at[pl.ds(1, 7)], rest_sem)
    total = stage[x // 2, 8 + x % 2].astype(F32)
    for by in range(1, 8):
        total += got_rest[by].astype(F32)
    gram[x // 2, pl.ds(pl.multiple_of(128 + 16 * (x % 2), 16), 16), :] = total.astype(BF16)
    spread_own(2)

    def image_chunk(a):
        images.settle(a)
        product = jnp.dot(
            gram[a], v_all[CHUNK * a : CHUNK * a + CHUNK, :], preferred_element_type=F32
        )
        if a == 0:
            w_acc[...] = product
        else:
            w_acc[...] += product

    for turn in range(1, 9):
        if turn < 5:
            if turn > 1:
                spread_hop(0, turn)
            spread_hop(1, turn)
            if turn == 4:
                spread_hop(2, turn)
            image_of(turn)
            if turn < 4:
                spread_hop(2, turn)
        if turn == 4:
            sums = jnp.zeros((8, 128), F32)
            for b in range(CHUNKS):
                values = gram[b].astype(F32)
                part = jnp.sum((values * values).reshape(20, 8, CHUNK), axis=0)
                for k in range(CHUNK // 128):
                    sums += part[:, 128 * k : 128 * k + 128]
            squares[0] = sums
            push(squares.at[0], squares.at[1], send_sems.at[9], square_sem.at[0], sibling)
        if turn == 5:
            wait(squares.at[1], square_sem.at[0])
            squares[2] = squares[0] + squares[1]
            for by in range(1, 8):
                push(squares.at[2], squares.at[2 + by], send_sems.at[10], square_sem.at[1], at_z(by))
        for hop in range(1, 5):
            if 0 <= turn - hop < SUBS:
                images.step(hop, turn - hop)
        if turn >= 5:
            image_chunk(turn - 5)

    wait(squares.at[pl.ds(3, 7)], square_sem.at[1])
    total = squares[2]
    for by in range(1, 8):
        total += squares[2 + by]
    square_sum = jnp.sum(total, keepdims=True)
    factor = lax.rsqrt(jnp.sqrt(square_sum / H + tiny_value))
    factor_2 = factor * factor
    result = (math.sqrt(D) * factor) * (
        first_coef * u_all[0:ROWS, :].astype(F32)
        + (third_coef * factor_2) * v_all[0:ROWS, :].astype(F32)
        + (fifth_coef * factor_2 * factor_2) * w_acc[...]
    )
    result = result.astype(BF16)
    for p in range(8):
        reply[ORDER[p], :, :COLS] = result[16 * p : 16 * p + 16, :]
    rest = jnp.zeros((128, 128), F32)
    for k in range(4):
        chosen = selection(
            (128, 32), lambda r: jnp.where(r % 16 // 4 == k, 4 * (r // 16) + r % 4, -1)
        )
        rest += pick(chosen, result[128:160, 128 * k : 128 * k + 128])
    reply[:, :, COLS:] = rest.astype(BF16).reshape(8, 16, 128)
    for by in FARTHEST_FIRST:
        push(reply.at[by], returned.at[y], send_sems.at[11], return_sem, at_y(-by))
    returned[y] = reply[0]
    wait(returned.at[pl.ds(0, 7)], return_sem)
    main = returned[:, :, :COLS].reshape(128, COLS)
    main = pick(selection((128, 128), lambda r: 16 * (r % 8) + r // 8), main)
    out_ref[0:16] = main.reshape(16, 8, COLS).astype(BF16)
    rest = returned[:, :, COLS:].reshape(128, 128)
    for k in range(4):
        chosen = selection((32, 128), lambda r: 16 * (r % 8) + 4 * k + r // 8)
        out_ref[16:20, :, 128 * k : 128 * k + 128] = (
            pick(chosen, rest).reshape(4, 8, 128).astype(BF16)
        )

    wait(arrived.at[pl.ds(1, 7)], send_sems.at[0])
    wait(u_all.at[pl.ds(0, 7 * ROWS)], send_sems.at[1])
    wait(u_all.at[pl.ds(0, 8 * ROWS)], send_sems.at[2])
    wait(v_all.at[pl.ds(0, 7 * ROWS)], send_sems.at[3])
    wait(v_all.at[pl.ds(0, 8 * ROWS)], send_sems.at[4])
    for a in range(CHUNKS):
        wait(got.at[a, pl.ds(1, 7)], send_sems.at[5])
    wait(got_rest.at[pl.ds(1, 7)], send_sems.at[5])
    for kind in range(3):
        for _ in range(7):
            wait(piece(kind, x), send_sems.at[6 + kind])
    wait(squares.at[0], send_sems.at[9])
    wait(squares.at[pl.ds(3, 7)], send_sems.at[10])
    wait(reply.at[pl.ds(1, 7)], send_sems.at[11])


def step(gradient, momentum, row_counts):
    DMA = pltpu.SemaphoreType.DMA
    return pl.pallas_call(
        kernel,
        out_shape=jax.ShapeDtypeStruct((20, 8, COLS), BF16),
        in_specs=[pl.BlockSpec(memory_space=pl.ANY)] * 3,
        out_specs=pl.BlockSpec(memory_space=pltpu.VMEM),
        scratch_shapes=[
            pltpu.VMEM((20, 8, COLS), BF16),
            pltpu.VMEM((20, 8, COLS), F32),
            pltpu.VMEM((8, 128), jnp.int32),
            pltpu.VMEM((8, 16, WIDE), BF16),
            pltpu.VMEM((8, 16, WIDE), BF16),
            pltpu.VMEM((FULL, COLS), BF16),
            pltpu.VMEM((FULL, COLS), BF16),
            pltpu.VMEM((CHUNKS, 10, 16, CHUNK), BF16),
            pltpu.VMEM((CHUNKS, 8, 16, CHUNK), BF16),
            pltpu.VMEM((8, 16, CHUNK), BF16),
            pltpu.VMEM((CHUNKS, ROWS, CHUNK), BF16),
            pltpu.VMEM((ROWS, COLS), F32),
            pltpu.VMEM((10, 8, 128), F32),
            pltpu.VMEM((8, 16, WIDE), BF16),
            pltpu.VMEM((8, 16, WIDE), BF16),
            DMA((3,)),
            DMA((12,)),
            DMA((8,)),
            DMA((2, 4, SUBS)),
            DMA((8,)),
            DMA((2, 4, SUBS)),
            DMA((8,)),
            DMA((CHUNKS,)),
            DMA,
            DMA((2, 4, 3)),
            DMA((2,)),
            DMA,
        ],
        compiler_params=pltpu.CompilerParams(
            collective_id=0, has_side_effects=True, vmem_limit_bytes=63 * 1024 * 1024
        ),
    )(gradient, momentum, row_counts)


def on_device(gradient, momentum, row_counts):
    new_momentum = keep_rate * momentum + gradient.astype(F32)
    result = step(gradient.transpose(1, 0, 2), momentum.transpose(1, 0, 2), row_counts)
    return (new_momentum, result.transpose(1, 0, 2).astype(F32))


def solution(mesh):
    placed = (P(None, "fsdp", "grp"), P(None, "fsdp", "grp"), P())
    return jax.shard_map(
        on_device,
        mesh=mesh,
        in_specs=placed,
        out_specs=(P(None, "fsdp", "grp"), P(None, "fsdp", "grp")),
        check_vma=False,
    )
```

time: 105 us -> 99 us (0.943)
  Pallas kernels: 99 us -> 95.6 us
  local copies, waits for them, and re-layouts: 2.64 us -> 0.01 us
    pallas_call x1, Pallas kernels: 99 us -> 95.6 us  [step(): pl.pallas_call(kernel, out_shape=jax.ShapeDtypeStruct((20, 8, COLS), BF16...]
    unnamed x8 -> x4, local copies, waits for them, and re-layouts: 2.6 us -> 0.01 us
    convert_element_type x1, other arithmetic: 0.04 us -> 1.73 us  [on_device(): return (new_momentum, result.transpose(1, 0, 2).astype(F32))]
    select_n x2 -> x0, other arithmetic: 1.54 us -> none  [the longest x1 1.36 us: on_device(): slots = jnp.where(live[:, :, None], nesterov, jnp.zeros_like(nesterov))]
where the time goes in v2:
time: 99 us; the launch traced here: 98.8 us
  Pallas kernels  95.6 us (97%)
  other arithmetic  2.5 us (3%)
    pallas_call x1, Pallas kernels, step(): pl.pallas_call(kernel, out_shape=jax.ShapeDtypeStruct((20, 8, COLS), BF16...  95.6 us

profile of v2, /device:TPU:1, one launch (start us, length us, event | category | flops | bytes accessed | tf_op | source)
XLA Modules:
  0.0 98.8 jit_solution(6035165040944292630)
XLA Ops:
  0.6 95.6 %shard_map.50 = bf16[20,8,512]{2,1,0:T(8,128)(2,1)} custom-call(bf16[20,8,512]{2,1,0:T(8,128)(2,1)} %bitcast.5, f32[20,8,512]{2,1,0:T(8,128)} %bitcast.4, s32[8,128]{1,0:T(8,128)} %counts_ref.1), custom_call_target="tpu_custom_call" | custom-call | tf_op jit(solution)/shard_map/pallas_call | solution.py:440
  96.2 0.0 copy-start
  96.3 0.0 copy-start.1
  96.3 1.7 %convert_bitcast_fusion = f32[8,20,512]{2,0,1:T(8,128)} fusion(bf16[20,8,512]{2,1,0:T(8,128)(2,1)} %shard_map.50), kind=kLoop, calls=%fused_computation | loop fusion | flops 81920 | bytes 491520 | tf_op jit(solution)/shard_map/convert_element_type | solution.py:483
  98.0 0.0 copy-done
  98.0 0.0 copy-done.1
  98.0 0.8 convert_add_fusion
Async XLA Ops:
  96.2 1.8 %copy-start = (f32[8,20,512]{2,0,1:T(8,128)S(1)}, f32[8,20,512]{2,0,1:T(8,128)}, u32[]{:S(2)}) copy-start(f32[8,20,512]{2,0,1:T(8,128)} %param.4) | copy-start | bytes 983044
  96.3 1.7 %copy-start.1 = (bf16[8,20,512]{2,0,1:T(8,128)(2,1)S(1)}, bf16[8,20,512]{2,0,1:T(8,128)(2,1)}, u32[]{:S(2)}) copy-start(bf16[8,20,512]{2,0,1:T(8,128)(2,1)} %param.3) | copy-start | bytes 491524

commit v3 on v2

--- a/solution.py
+++ b/solution.py
@@ -27,6 +27,11 @@
 PLACE = {0: 0, -1: 1, 1: 2, -2: 3, 2: 4, -3: 5, 3: 6, 4: 7}
 ORDER = (0, 1, 7, 2, 6, 3, 5, 4)
 FARTHEST_FIRST = (4, 3, 5, 2, 6, 1, 7)
+NEAREST_FIRST = (1, 7, 2, 6, 3, 5, 4)
+SHORT_U = ()
+SHORT_V = (3, 4)
+SHORT_X = (2, 3)
+LAST_WAY_X = (0, 1, 1, 0)
 F32 = jnp.float32
 BF16 = jnp.bfloat16
 
@@ -103,20 +108,21 @@
     def wait(ref, sem):
         pltpu.make_async_copy(ref, ref, sem).wait()
 
+    fetches = [
+        pltpu.make_async_copy(src, dst, local_sem.at[i])
+        for i, (src, dst) in enumerate(
+            ((gradient_ref, gradient), (momentum_ref, momentum), (counts_ref, counts))
+        )
+    ]
+    for fetch in fetches:
+        fetch.start()
+
     barrier = pltpu.get_barrier_semaphore()
     for by in range(1, 8):
         for peer in (at_y(by), at_z(by), at_x(by)):
             pl.semaphore_signal(barrier, inc=1, device_id=peer, device_id_type=MESH)
     pl.semaphore_signal(barrier, inc=1, device_id=sibling, device_id_type=MESH)
 
-    fetches = [
-        pltpu.make_async_copy(src, dst, local_sem.at[i])
-        for i, (src, dst) in enumerate(
-            ((gradient_ref, gradient), (momentum_ref, momentum), (counts_ref, counts))
-        )
-    ]
-    for fetch in fetches:
-        fetch.start()
     for fetch in fetches:
         fetch.wait()
     grad = gradient[...].astype(F32)
@@ -138,7 +144,8 @@
     pl.semaphore_wait(barrier, 22)
 
     class Ring:
-        def __init__(self, buf, parts, ring_sem, sib_sem, ring_send, sib_send):
+        def __init__(self, buf, parts, short, ring_sem, sib_sem, ring_send, sib_send):
+            self.short = short
             self.buf, self.parts = buf, parts
             self.ring_sem, self.sib_sem = ring_sem, sib_sem
             self.ring_send, self.sib_send = ring_send, sib_send
@@ -153,8 +160,8 @@
         def place(self, way, hop):
             return PLACE[4 if hop == 4 else (-hop if way == 0 else hop)]
 
-        def forward(self, way, hop, sub):
-            source = 0 if hop == 1 else self.place(way, hop - 1)
+        def forward(self, way, hop, sub, chips=1):
+            source = 0 if hop == chips else self.place(way, hop - chips)
             for src, dst in zip(
                 self.refs(source, 0, sub), self.refs(self.place(way, hop), 0, sub), strict=True
             ):
@@ -163,7 +170,7 @@
                     dst,
                     self.ring_send,
                     self.ring_sem.at[way, hop - 1, sub],
-                    at_z(1 if way == 0 else -1),
+                    at_z(chips if way == 0 else -chips),
                 )
 
         def twin(self, place, sub):
@@ -172,6 +179,8 @@
 
         def send_own(self, sub):
             for way in range(2):
+                if sub in self.short:
+                    self.forward(way, 2, sub, 2)
                 self.forward(way, 1, sub)
             self.twin(0, sub)
 
@@ -182,7 +191,12 @@
                 if hop == 4 and way != last_way:
                     continue
                 wait(self.buf.at[pl.ds(0, size)], self.ring_sem.at[way, hop - 1, sub])
-                if hop < 3 or (hop == 3 and way == last_way):
+                if sub in self.short:
+                    if hop == 2:
+                        if way == last_way:
+                            self.forward(way, 4, sub, 2)
+                        self.forward(way, 3, sub)
+                elif hop < 3 or (hop == 3 and way == last_way):
                     self.forward(way, hop + 1, sub)
                 self.twin(self.place(way, hop), sub)
 
@@ -194,6 +208,7 @@
     whole = Ring(
         u_all,
         [[(0, 16)], [(16, 32)], [(48, 32)], [(80, 48)], [(128, 32)]],
+        SHORT_U,
         ring_u,
         sib_u,
         send_sems.at[1],
@@ -204,6 +219,7 @@
         [[(group[0], 16)]]
         + [[(group[q], 16), (group[-q], 16)] for q in (1, 2, 3)]
         + [[(group[4], 16), (128, 32)]],
+        SHORT_V,
         ring_v,
         sib_v,
         send_sems.at[3],
@@ -220,35 +236,42 @@
         gram[a, own_rows, :] = total.astype(BF16)
 
     def piece(kind, owner):
-        if kind == 2:
+        if kind == 3:
             return gram.at[owner // 2, pl.ds(pl.multiple_of(128 + 16 * (owner % 2), 16), 16)]
-        return gram.at[pl.ds(2 * kind, 2), pl.ds(pl.multiple_of(16 * owner, 16), 16)]
+        first, chunks = ((0, 2), (2, 1), (3, 1))[kind]
+        return gram.at[pl.ds(first, chunks), pl.ds(pl.multiple_of(16 * owner, 16), 16)]
+
+    def spread(kind, way, hop, chips=1):
+        far = hop - chips
+        owner = (x - far) % 8 if way == 0 else (x + far) % 8
+        push(
+            piece(kind, owner),
+            piece(kind, owner),
+            send_sems.at[6 + kind],
+            spread_sem.at[way, hop - 1, kind],
+            at_x(chips if way == 0 else -chips),
+        )
 
     def spread_own(kind):
         for way in range(2):
-            push(
-                piece(kind, x),
-                piece(kind, x),
-                send_sems.at[6 + kind],
-                spread_sem.at[way, 0, kind],
-                at_x(1 if way == 0 else -1),
-            )
+            if kind in SHORT_X:
+                spread(kind, way, 2, 2)
+            spread(kind, way, 1)
 
     def spread_hop(kind, hop):
-        last_way = (0, 1, 0)[kind]
+        last_way = LAST_WAY_X[kind]
         for way in range(2):
             if hop == 4 and way != last_way:
                 continue
             owner = (x - hop) % 8 if way == 0 else (x + hop) % 8
             wait(piece(kind, owner), spread_sem.at[way, hop - 1, kind])
-            if hop < 3 or (hop == 3 and way == last_way):
-                push(
-                    piece(kind, owner),
-                    piece(kind, owner),
-                    send_sems.at[6 + kind],
-                    spread_sem.at[way, hop, kind],
-                    at_x(1 if way == 0 else -1),
-                )
+            if kind in SHORT_X:
+                if hop == 2:
+                    if way == last_way:
+                        spread(kind, way, 4, 2)
+                    spread(kind, way, 3)
+            elif hop < 3 or (hop == 3 and way == last_way):
+                spread(kind, way, hop + 1)
 
     def gram_chunk(a):
         whole.settle(a)
@@ -280,7 +303,7 @@
                     (f, owner),
                 )
 
-    for by in FARTHEST_FIRST:
+    for by in NEAREST_FIRST:
         push(message.at[(y + by) % 8], arrived.at[by], send_sems.at[0], owner_sem.at[by], at_y(by))
     arrived[0] = message[y]
     u_all[0:16, :] = arrived[0, :, :COLS]
@@ -314,8 +337,10 @@
 
     spread_hop(0, 1)
     reduce_chunk(2)
+    spread_own(1)
+    spread_hop(0, 2)
     reduce_chunk(3)
-    spread_own(1)
+    spread_own(2)
 
     def image_of(sub):
         parts = [
@@ -335,13 +360,13 @@
             done += part.size
         images.send_own(sub)
 
-    image_of(0)
     wait(got_rest.at[pl.ds(1, 7)], rest_sem)
     total = stage[x // 2, 8 + x % 2].astype(F32)
     for by in range(1, 8):
         total += got_rest[by].astype(F32)
     gram[x // 2, pl.ds(pl.multiple_of(128 + 16 * (x % 2), 16), 16), :] = total.astype(BF16)
-    spread_own(2)
+    spread_own(3)
+    image_of(0)
 
     def image_chunk(a):
         images.settle(a)
@@ -355,14 +380,15 @@
 
     for turn in range(1, 9):
         if turn < 5:
-            if turn > 1:
-                spread_hop(0, turn)
             spread_hop(1, turn)
-            if turn == 4:
-                spread_hop(2, turn)
+            spread_hop(2, turn)
+            if turn in (2, 4):
+                spread_hop(3, turn)
             image_of(turn)
-            if turn < 4:
-                spread_hop(2, turn)
+            if turn in (1, 3):
+                spread_hop(3, turn)
+            if turn < 3:
+                spread_hop(0, turn + 2)
         if turn == 4:
             sums = jnp.zeros((8, 128), F32)
             for b in range(CHUNKS):
@@ -371,12 +397,12 @@
                 for k in range(CHUNK // 128):
                     sums += part[:, 128 * k : 128 * k + 128]
             squares[0] = sums
-            push(squares.at[0], squares.at[1], send_sems.at[9], square_sem.at[0], sibling)
+            push(squares.at[0], squares.at[1], send_sems.at[10], square_sem.at[0], sibling)
         if turn == 5:
             wait(squares.at[1], square_sem.at[0])
             squares[2] = squares[0] + squares[1]
             for by in range(1, 8):
-                push(squares.at[2], squares.at[2 + by], send_sems.at[10], square_sem.at[1], at_z(by))
+                push(squares.at[2], squares.at[2 + by], send_sems.at[11], square_sem.at[1], at_z(by))
         for hop in range(1, 5):
             if 0 <= turn - hop < SUBS:
                 images.step(hop, turn - hop)
@@ -406,7 +432,7 @@
         rest += pick(chosen, result[128:160, 128 * k : 128 * k + 128])
     reply[:, :, COLS:] = rest.astype(BF16).reshape(8, 16, 128)
     for by in FARTHEST_FIRST:
-        push(reply.at[by], returned.at[y], send_sems.at[11], return_sem, at_y(-by))
+        push(reply.at[by], returned.at[y], send_sems.at[12], return_sem, at_y(-by))
     returned[y] = reply[0]
     wait(returned.at[pl.ds(0, 7)], return_sem)
     main = returned[:, :, :COLS].reshape(128, COLS)
@@ -427,12 +453,12 @@
     for a in range(CHUNKS):
         wait(got.at[a, pl.ds(1, 7)], send_sems.at[5])
     wait(got_rest.at[pl.ds(1, 7)], send_sems.at[5])
-    for kind in range(3):
+    for kind in range(4):
         for _ in range(7):
             wait(piece(kind, x), send_sems.at[6 + kind])
-    wait(squares.at[0], send_sems.at[9])
-    wait(squares.at[pl.ds(3, 7)], send_sems.at[10])
-    wait(reply.at[pl.ds(1, 7)], send_sems.at[11])
+    wait(squares.at[0], send_sems.at[10])
+    wait(squares.at[pl.ds(3, 7)], send_sems.at[11])
+    wait(reply.at[pl.ds(1, 7)], send_sems.at[12])
 
 
 def step(gradient, momentum, row_counts):
@@ -459,7 +485,7 @@
             pltpu.VMEM((8, 16, WIDE), BF16),
             pltpu.VMEM((8, 16, WIDE), BF16),
             DMA((3,)),
-            DMA((12,)),
+            DMA((13,)),
             DMA((8,)),
             DMA((2, 4, SUBS)),
             DMA((8,)),
@@ -467,7 +493,7 @@
             DMA((8,)),
             DMA((CHUNKS,)),
             DMA,
-            DMA((2, 4, 3)),
+            DMA((2, 4, 4)),
             DMA((2,)),
             DMA,
         ],

time: 99 us -> 97.8 us (0.988)
  Pallas kernels: 95.6 us -> 94.5 us
    pallas_call x1, Pallas kernels: 95.6 us -> 94.5 us  [step(): pl.pallas_call(kernel, out_shape=jax.ShapeDtypeStruct((20, 8, COLS), BF16...]
where the time goes in v3:
time: 97.8 us; the launch traced here: 97.7 us
  Pallas kernels  94.5 us (97%)
  other arithmetic  2.5 us (3%)
    pallas_call x1, Pallas kernels, step(): pl.pallas_call(kernel, out_shape=jax.ShapeDtypeStruct((20, 8, COLS), BF16...  94.5 us

profile of v3, /device:TPU:1, one launch (start us, length us, event | category | flops | bytes accessed | tf_op | source)
XLA Modules:
  0.0 97.7 jit_solution(7862526543202385558)
XLA Ops:
  0.6 94.5 %shard_map.50 = bf16[20,8,512]{2,1,0:T(8,128)(2,1)} custom-call(bf16[20,8,512]{2,1,0:T(8,128)(2,1)} %bitcast.5, f32[20,8,512]{2,1,0:T(8,128)} %bitcast.4, s32[8,128]{1,0:T(8,128)} %counts_ref.1), custom_call_target="tpu_custom_call" | custom-call | tf_op jit(solution)/shard_map/pallas_call | solution.py:466
  95.1 0.0 copy-start
  95.1 0.0 copy-start.1
  95.2 1.7 %convert_bitcast_fusion = f32[8,20,512]{2,0,1:T(8,128)} fusion(bf16[20,8,512]{2,1,0:T(8,128)(2,1)} %shard_map.50), kind=kLoop, calls=%fused_computation | loop fusion | flops 81920 | bytes 491520 | tf_op jit(solution)/shard_map/convert_element_type | solution.py:509
  96.9 0.0 copy-done
  96.9 0.0 copy-done.1
  96.9 0.8 convert_add_fusion
Async XLA Ops:
  95.1 1.8 %copy-start = (f32[8,20,512]{2,0,1:T(8,128)S(1)}, f32[8,20,512]{2,0,1:T(8,128)}, u32[]{:S(2)}) copy-start(f32[8,20,512]{2,0,1:T(8,128)} %param.4) | copy-start | bytes 983044
  95.1 1.7 %copy-start.1 = (bf16[8,20,512]{2,0,1:T(8,128)(2,1)S(1)}, bf16[8,20,512]{2,0,1:T(8,128)(2,1)}, u32[]{:S(2)}) copy-start(bf16[8,20,512]{2,0,1:T(8,128)(2,1)} %param.3) | copy-start | bytes 491524

commit v4 on v3

--- a/solution.py
+++ b/solution.py
@@ -503,10 +503,18 @@
     )(gradient, momentum, row_counts)
 
 
+def finish(result_ref, gradient_ref, momentum_ref, new_ref, update_ref):
+    new_ref[...] = keep_rate * momentum_ref[...] + gradient_ref[...].astype(F32)
+    update_ref[...] = result_ref[...].astype(F32)
+
+
 def on_device(gradient, momentum, row_counts):
-    new_momentum = keep_rate * momentum + gradient.astype(F32)
-    result = step(gradient.transpose(1, 0, 2), momentum.transpose(1, 0, 2), row_counts)
-    return (new_momentum, result.transpose(1, 0, 2).astype(F32))
+    gradient, momentum = gradient.transpose(1, 0, 2), momentum.transpose(1, 0, 2)
+    result = step(gradient, momentum, row_counts)
+    new_momentum, update = pl.pallas_call(
+        finish, out_shape=(jax.ShapeDtypeStruct(momentum.shape, F32),) * 2
+    )(result, gradient, momentum)
+    return (new_momentum.transpose(1, 0, 2), update.transpose(1, 0, 2))
 
 
 def solution(mesh):

time: 97.8 us -> 97.3 us (level)
  other arithmetic: 2.5 us -> 0 us
  Pallas kernels: 94.5 us -> 96.5 us
    pallas_call x0 -> x1, Pallas kernels: none -> 2.01 us  [on_device(): pl.pallas_call(finish, out_shape=(jax.ShapeDtypeStruct(momentum.shape, F3...]
    convert_element_type x1 -> x0, other arithmetic: 1.73 us -> none  [on_device(): return (new_momentum, result.transpose(1, 0, 2).astype(F32))]
where the time goes in v4:
time: 97.3 us; the launch traced here: 97.1 us
  Pallas kernels  96.5 us (99%)
    pallas_call x1, Pallas kernels, step(): pl.pallas_call(kernel, out_shape=jax.ShapeDtypeStruct((20, 8, COLS), BF16...  94.5 us
    pallas_call x1, Pallas kernels, on_device(): pl.pallas_call(finish, out_shape=(jax.ShapeDtypeStruct(momentum.shape, F3...  2.01 us

profile of v4, /device:TPU:1, one launch (start us, length us, event | category | flops | bytes accessed | tf_op | source)
XLA Modules:
  0.0 97.1 jit_solution(596907609667512798)
XLA Ops:
  0.6 94.5 %shard_map.50.result_ref = bf16[20,8,512]{2,1,0:T(8,128)(2,1)} custom-call(bf16[20,8,512]{2,1,0:T(8,128)(2,1)} %bitcast.6, f32[20,8,512]{2,1,0:T(8,128)} %bitcast.4, s32[8,128]{1,0:T(8,128)} %counts_ref.1), custom_call_target="tpu_custom_call" | custom-call | tf_op jit(solution)/shard_map/pallas_call | solution.py:466
  95.1 2.0 %shard_map.51 = (f32[20,8,512]{2,1,0:T(8,128)}, f32[20,8,512]{2,1,0:T(8,128)}) custom-call(bf16[20,8,512]{2,1,0:T(8,128)(2,1)} %shard_map.50.result_ref, bf16[20,8,512]{2,1,0:T(8,128)(2,1)} %bitcast.7, f32[20,8,512]{2,1,0:T(8,128)} %bitcast.5), custom_call_target="tpu_custom_call" | custom-call | tf_op jit(solution)/shard_map/pallas_call | solution.py:514
